TPU v7x, 256 devices: a whole 4x4x8 slice. The times are simulated.
256 devices in a mesh: row: 16 (over x, y), col: 16 (over z, core).
Axes of the slice: x: 4, y: 4, z: 8, core: 2. Of those that a mesh axis runs over, the one named last changes fastest.
Arguments:
- tokens: bfloat16 [131072, 128], P('row'), may hold values from -6 to 6
- centroids: bfloat16 [65536, 128], P('col'), may hold values from -6 to 6
- row_mass: float32 [131072], P('row'), may hold values from 0.25 to 4
- col_mass: float32 [65536], P('col'), may hold values from 0.25 to 4
- candidates: int32 [1024, 64], P('row', 'col'), may hold values from 0 to 31, as said below
- counts: int32 [1024, 16], P('row', 'col'), may hold values from 1 to 4, as said below
Outputs:
- query_term_dual_variable: float32 [131072], P('row')
- cluster_dual_variable: float32 [65536], P('col')
- barycenter: bfloat16 [131072, 128], P('row')
Inputs may be any that keep to these rules, and one draw needn't show every extreme that they name: `candidates`: for token tile t and column shard c, entries c * 4 to c * 4 + counts[t, c] - 1 of row t are distinct local tile numbers of that shard and the remaining entries of that group are 0. Every centroid tile is listed by some token tile. `counts`: every token tile lists at least one tile of every column shard; the most listed for one token tile and shard is 4, reached in every draw.
All inputs are finite; a program needn't handle non-finite values.
Results may differ from a plain program's by a relative error of at most 0.0081.
Values may be sent and summed in bfloat16 or wider, within the bound.
A program may use at most 64 MiB of HBM per device.

v0:
```python
import jax
import jax.numpy as jnp
from jax import lax
from jax.sharding import PartitionSpec as P

TILE = 128
SLOTS = 4
ITERS = 2


entropic_regularizer = 0.025
square_start_position = 0.5


def unit_rows(values):
    widened = values.astype(jnp.float32)
    factor = lax.rsqrt(jnp.mean(widened * widened, axis=-1, keepdims=True) + 1e-06)
    return (widened * factor).astype(jnp.bfloat16)


def shards(tokens, centroids, row_mass, col_mass, candidates, counts):
    query_term_vectors = tokens.shape[1]
    token_blocks = unit_rows(tokens).reshape(-1, TILE, query_term_vectors)
    centroid_blocks = unit_rows(centroids).reshape(-1, TILE, query_term_vectors)
    token_count = token_blocks.shape[0]
    centroid_count = centroid_blocks.shape[0]
    listed = counts[:, 0]
    tile_numbers = jnp.arange(centroid_count, dtype=jnp.int32)
    slot_limit = SLOTS

    def slot_kernel(slot_index):
        chosen = lax.dynamic_index_in_dim(candidates, slot_index, 1, keepdims=False)
        active = slot_index < listed
        picked = jnp.take(centroid_blocks, chosen, axis=0)
        similarity_values = jnp.einsum(
            "bad,bcd->bac", token_blocks, picked, preferred_element_type=jnp.float32
        )
        gibbs_similarity_matrix = jnp.exp(
            (similarity_values / query_term_vectors - square_start_position) / entropic_regularizer
        )
        gibbs_similarity_matrix = jnp.where(
            active[:, None, None], gibbs_similarity_matrix, jnp.zeros_like(gibbs_similarity_matrix)
        )
        return (chosen, picked, gibbs_similarity_matrix)

    target_linear_position = jnp.ones((centroid_count * TILE,), jnp.float32)
    source_linear_position = jnp.ones((token_count * TILE,), jnp.float32)
    for sweep_index in range(ITERS):
        row_target_square_numbers = target_linear_position.reshape(centroid_count, TILE)

        def row_advance(slot_index, totals):
            chosen, picked, gibbs_similarity_matrix = slot_kernel(slot_index)
            scales = jnp.take(row_target_square_numbers, chosen, axis=0)
            return totals + jnp.einsum(
                "bac,bc->ba", gibbs_similarity_matrix, scales, precision=lax.Precision.HIGHEST
            )

        row_start = jnp.zeros((token_count, TILE), jnp.float32)
        source_linear_position = row_mass / lax.psum(
            lax.fori_loop(0, slot_limit, row_advance, row_start).reshape(-1), "col"
        )
        col_source_square_numbers = source_linear_position.reshape(token_count, TILE)

        def col_advance(slot_index, totals):
            chosen, picked, gibbs_similarity_matrix = slot_kernel(slot_index)
            partial_value = jnp.einsum(
                "bac,ba->bc",
                gibbs_similarity_matrix,
                col_source_square_numbers,
                precision=lax.Precision.HIGHEST,
            )
            one_hot = (chosen[:, None] == tile_numbers[None, :]).astype(jnp.float32)
            return totals + jnp.einsum(
                "bn,bc->nc", one_hot, partial_value, precision=lax.Precision.HIGHEST
            )

        col_start = jnp.zeros((centroid_count, TILE), jnp.float32)
        target_linear_position = col_mass / lax.psum(
            lax.fori_loop(0, slot_limit, col_advance, col_start).reshape(-1), "row"
        )
    source_square_numbers = source_linear_position.reshape(token_count, TILE)
    target_square_numbers = target_linear_position.reshape(centroid_count, TILE)

    def gather_plan(slot_index, carried):
        numerator, denominator = carried
        chosen, picked, gibbs_similarity_matrix = slot_kernel(slot_index)
        plan = (
            gibbs_similarity_matrix
            * source_square_numbers[:, :, None]
            * jnp.take(target_square_numbers, chosen, axis=0)[:, None, :]
        )
        denominator = denominator + jnp.sum(plan, axis=2)
        numerator = numerator + jnp.einsum(
            "bac,bcd->bad", plan.astype(jnp.bfloat16), picked, preferred_element_type=jnp.float32
        )
        return (numerator, denominator)

    start = (
        jnp.zeros((token_count, TILE, query_term_vectors), jnp.float32),
        jnp.zeros((token_count, TILE), jnp.float32),
    )
    numerator, denominator = lax.fori_loop(0, slot_limit, gather_plan, start)
    numerator = numerator.reshape(-1, query_term_vectors)
    denominator = denominator.reshape(-1)
    num_whole, den_whole = lax.psum((numerator, denominator), "col")
    barycenter = (num_whole / den_whole[:, None]).astype(jnp.bfloat16)
    query_term_dual_variable = entropic_regularizer * jnp.log(source_linear_position)
    cluster_dual_variable = entropic_regularizer * jnp.log(target_linear_position)
    return (query_term_dual_variable, cluster_dual_variable, barycenter)


def solution(mesh):
    in_specs = (
        P("row", None),
        P("col", None),
        P("row"),
        P("col"),
        P("row", "col"),
        P("row", "col"),
    )
    out_specs = (P("row"), P("col"), P("row", None))
    return jax.shard_map(shards, mesh=mesh, in_specs=in_specs, out_specs=out_specs, check_vma=False)
```

profile of v0, /device:TPU:1, one launch (start us, length us, event | category | flops | bytes accessed | tf_op | source)
XLA Modules:
  0.0 625.3 jit_solution(5814523411643270381)
XLA Ops:
  17.4 42.1 %while.82 = (s32[]{:T(128)}, f32[64,128]{1,0:T(8,128)S(1)}, s32[64]{0:T(128)S(1)}, s32[64,4]{0,1:T(4,128)S(1)}, bf16[32,128,128]{2,1,0:T(8,128)(2,1)S(1)}, /*ind...) while((s32[]{:T(128)}, f32[64,128]{1,0:T(8,128)S(1)}, s32[64]{0:T(128)S(1)}, ...), condition=%wide.region_3.6_spmd.clone, body=%wide.region_2.5_spmd.clone.sunk | while | flops 286287296 | bytes 17095600 | solution.py:60
  23.5 4.4 fusion.147
  34.0 4.4 fusion.147
  44.5 4.4 fusion.147
  55.1 4.4 fusion.147
  59.5 48.8 %psum.42 = f32[8192]{0:T(1024)S(1)} all-reduce(f32[8192]{0:T(1024)S(1)} %bitcast.116), channel_id=1, replica_groups=mesh['row'=16,'col'=16] {'col'}, use_global_device_ids=true, to_apply=%region_4.7 | all-reduce | flops 8192 | bytes 65536 | tf_op jit(solution)/shard_map/psum | solution.py:59
  108.3 51.3 %while.83 = (s32[]{:T(128)}, f32[32,128]{1,0:T(8,128)S(1)}, s32[64,4]{0,1:T(4,128)S(1)}, s32[64]{0:T(128)S(1)}, bf16[32,128,128]{2,1,0:T(8,128)(2,1)S(1)}, /*ind...) while((s32[]{:T(128)}, f32[32,128]{1,0:T(8,128)S(1)}, ...), condition=%wide.region_6.9_spmd.clone, body=%wide.region_5.8_spmd.clone.sunk | while | flops 289418880 | bytes 16915820 | solution.py:79
  113.7 7.1 %fusion.154 = f32[64,1,128]{2,1,0:T(1,128)S(1)} fusion(f32[64,128,1]{1,2,0:T(1,128)S(1)} %bitcast.126, f32[64,128,128]{2,1,0:T(8,128)S(1)} %fusion.153, pred[64]{0:T(512)(128)(4,1)S(1)} %get-tuple-element.1398), kind=kOutput, calls=%fused_computation.36.clone.1 | convolution fusion | flops 16777216 | bytes 4259904 | tf_op jit(solution)/shard_map/while/body/eval_jaxpr/bac,ba->bc/dot_general | solution.py:66
  126.6 7.1 %fusion.154 = f32[64,1,128]{2,1,0:T(1,128)S(1)} fusion(f32[64,128,1]{1,2,0:T(1,128)S(1)} %bitcast.126, f32[64,128,128]{2,1,0:T(8,128)S(1)} %fusion.153, pred[64]{0:T(512)(128)(4,1)S(1)} %get-tuple-element.1398), kind=kOutput, calls=%fused_computation.36.clone.1 | convolution fusion | flops 16777216 | bytes 4259904 | tf_op jit(solution)/shard_map/while/body/eval_jaxpr/bac,ba->bc/dot_general | solution.py:66
  139.4 7.1 %fusion.154 = f32[64,1,128]{2,1,0:T(1,128)S(1)} fusion(f32[64,128,1]{1,2,0:T(1,128)S(1)} %bitcast.126, f32[64,128,128]{2,1,0:T(8,128)S(1)} %fusion.153, pred[64]{0:T(512)(128)(4,1)S(1)} %get-tuple-element.1398), kind=kOutput, calls=%fused_computation.36.clone.1 | convolution fusion | flops 16777216 | bytes 4259904 | tf_op jit(solution)/shard_map/while/body/eval_jaxpr/bac,ba->bc/dot_general | solution.py:66
  152.2 7.1 %fusion.154 = f32[64,1,128]{2,1,0:T(1,128)S(1)} fusion(f32[64,128,1]{1,2,0:T(1,128)S(1)} %bitcast.126, f32[64,128,128]{2,1,0:T(8,128)S(1)} %fusion.153, pred[64]{0:T(512)(128)(4,1)S(1)} %get-tuple-element.1398), kind=kOutput, calls=%fused_computation.36.clone.1 | convolution fusion | flops 16777216 | bytes 4259904 | tf_op jit(solution)/shard_map/while/body/eval_jaxpr/bac,ba->bc/dot_general | solution.py:66
  159.7 60.7 %psum.43 = f32[4096]{0:T(1024)S(1)} all-reduce(f32[4096]{0:T(1024)S(1)} %bitcast.124), channel_id=1, replica_groups=mesh['row'=16,'col'=16] {'row'}, use_global_device_ids=true, to_apply=%region_7.10 | all-reduce | flops 4096 | bytes 32768 | tf_op jit(solution)/shard_map/psum | solution.py:78
  220.4 42.1 %while.84 = (s32[]{:T(128)}, f32[64,128]{1,0:T(8,128)S(1)}, s32[64]{0:T(128)S(1)}, s32[64,4]{0,1:T(4,128)S(1)}, bf16[32,128,128]{2,1,0:T(8,128)(2,1)S(1)}, /*ind...) while((s32[]{:T(128)}, f32[64,128]{1,0:T(8,128)S(1)}, ...), condition=%wide.region_9.12_spmd.clone, body=%wide.region_8.11_spmd.clone.sunk | while | flops 286287296 | bytes 17079212 | solution.py:60
  226.5 4.4 fusion.160
  237.0 4.4 fusion.160
  247.5 4.4 fusion.160
  258.1 4.4 fusion.160
  262.5 59.8 %psum.44 = f32[8192]{0:T(1024)S(1)} all-reduce(f32[8192]{0:T(1024)S(1)} %bitcast.115), channel_id=1, replica_groups=mesh['row'=16,'col'=16] {'col'}, use_global_device_ids=true, to_apply=%region_10.13 | all-reduce | flops 8192 | bytes 65536 | tf_op jit(solution)/shard_map/psum | solution.py:59
  323.0 51.3 %while.85 = (s32[]{:T(128)}, f32[32,128]{1,0:T(8,128)S(1)}, s32[64,4]{0,1:T(4,128)S(1)}, s32[64]{0:T(128)S(1)}, bf16[32,128,128]{2,1,0:T(8,128)(2,1)S(1)}, /*ind...) while((s32[]{:T(128)}, f32[32,128]{1,0:T(8,128)S(1)}, ...), condition=%wide.region_12.15_spmd.clone, body=%wide.region_11.14_spmd.clone.sunk | while | flops 289418880 | bytes 16915820 | solution.py:79
  328.3 7.1 %fusion.167 = f32[64,1,128]{2,1,0:T(1,128)S(1)} fusion(f32[64,128,1]{1,2,0:T(1,128)S(1)} %bitcast.128, f32[64,128,128]{2,1,0:T(8,128)S(1)} %fusion.166, pred[64]{0:T(512)(128)(4,1)S(1)} %get-tuple-element.1418), kind=kOutput, calls=%fused_computation.90.clone.1 | convolution fusion | flops 16777216 | bytes 4259904 | tf_op jit(solution)/shard_map/while/body/eval_jaxpr/bac,ba->bc/dot_general | solution.py:66
  341.2 7.1 %fusion.167 = f32[64,1,128]{2,1,0:T(1,128)S(1)} fusion(f32[64,128,1]{1,2,0:T(1,128)S(1)} %bitcast.128, f32[64,128,128]{2,1,0:T(8,128)S(1)} %fusion.166, pred[64]{0:T(512)(128)(4,1)S(1)} %get-tuple-element.1418), kind=kOutput, calls=%fused_computation.90.clone.1 | convolution fusion | flops 16777216 | bytes 4259904 | tf_op jit(solution)/shard_map/while/body/eval_jaxpr/bac,ba->bc/dot_general | solution.py:66
  354.0 7.1 %fusion.167 = f32[64,1,128]{2,1,0:T(1,128)S(1)} fusion(f32[64,128,1]{1,2,0:T(1,128)S(1)} %bitcast.128, f32[64,128,128]{2,1,0:T(8,128)S(1)} %fusion.166, pred[64]{0:T(512)(128)(4,1)S(1)} %get-tuple-element.1418), kind=kOutput, calls=%fused_computation.90.clone.1 | convolution fusion | flops 16777216 | bytes 4259904 | tf_op jit(solution)/shard_map/while/body/eval_jaxpr/bac,ba->bc/dot_general | solution.py:66
  366.9 7.1 %fusion.167 = f32[64,1,128]{2,1,0:T(1,128)S(1)} fusion(f32[64,128,1]{1,2,0:T(1,128)S(1)} %bitcast.128, f32[64,128,128]{2,1,0:T(8,128)S(1)} %fusion.166, pred[64]{0:T(512)(128)(4,1)S(1)} %get-tuple-element.1418), kind=kOutput, calls=%fused_computation.90.clone.1 | convolution fusion | flops 16777216 | bytes 4259904 | tf_op jit(solution)/shard_map/while/body/eval_jaxpr/bac,ba->bc/dot_general | solution.py:66
  374.3 55.7 %psum.45 = f32[4096]{0:T(1024)S(1)} all-reduce(f32[4096]{0:T(1024)S(1)} %bitcast.123), channel_id=1, replica_groups=mesh['row'=16,'col'=16] {'row'}, use_global_device_ids=true, to_apply=%region_13.16 | all-reduce | flops 4096 | bytes 32768 | tf_op jit(solution)/shard_map/psum | solution.py:78
  430.6 53.2 %while.86 = (s32[]{:T(128)}, f32[64,128,128]{2,1,0:T(8,128)}, f32[64,128]{1,0:T(8,128)S(1)}, s32[64]{0:T(128)S(1)}, s32[64,4]{0,1:T(4,128)S(1)}, /*index=5*/bf16...) while((s32[]{:T(128)}, f32[64,128,128]{2,1,0:T(8,128)}, ...), condition=%wide.region_16.19_spmd.clone, body=%wide.region_14.18_spmd.clone.sunk | while | flops 555763136 | bytes 69606544 | solution.py:102
  433.4 4.5 bitcast_reduce_fusion.2
  437.9 4.0 select_add_fusion.10
  446.7 4.5 bitcast_reduce_fusion.2
  460.0 4.5 bitcast_reduce_fusion.2
  473.3 4.5 bitcast_reduce_fusion.2
  483.8 59.6 %psum.47 = f32[8192]{0:T(1024)S(1)} all-reduce(f32[8192]{0:T(1024)S(1)} %bitcast.114), channel_id=1, replica_groups=mesh['row'=16,'col'=16] {'col'}, use_global_device_ids=true, to_apply=%region_18.21 | all-reduce | flops 8192 | bytes 65536 | tf_op jit(solution)/shard_map/psum | solution.py:105
  543.4 71.2 %all-reduce.2.cloned.1.call-done = f32[8192,128]{1,0:T(8,128)} async-done(((f32[8192,128]{1,0:T(8,128)}), f32[8192,128]{1,0:T(8,128)}) %all-reduce.2.cloned.1.call-update) | async-done | bytes 4194320 | tf_op jit(solution)/shard_map/psum | solution.py:105
  (188 shorter events, 139.9 us)
Async XLA Ops:
  7.2 607.5 %all-reduce.2.cloned.1.call-start = ((), (), s32[]{:S(2)}) async-start(), calls=%async_computation | async-start | bytes 8388608 | tf_op jit(solution)/shard_map/psum | solution.py:105
  7.3 6.6 %copy-start.1 = (bf16[8192,128]{1,0:T(8,128)(2,1)S(1)}, bf16[8192,128]{1,0:T(8,128)(2,1)}, u32[]{:S(2)}) copy-start(bf16[8192,128]{1,0:T(8,128)(2,1)} %param.20) | copy-start | bytes 6291460
  9.3 8.1 %copy-start.4 = (s32[64,1]{0,1:T(1,128)S(1)}, s32[64,1]{0,1:T(1,128)}, u32[]{:S(2)}) copy-start(s32[64,1]{0,1:T(1,128)} %param.25) | copy-start | bytes 772
  9.3 8.1 %copy-start.6 = (s32[64,4]{0,1:T(4,128)S(1)}, s32[64,4]{0,1:T(4,128)}, u32[]{:S(2)}) copy-start(s32[64,4]{0,1:T(4,128)} %param.24) | copy-start | bytes 3076
  17.4 90.9 %copy-start.5 = (f32[8192]{0:T(1024)S(1)}, f32[8192]{0:T(1024)}, u32[]{:S(2)}) copy-start(f32[8192]{0:T(1024)} %param.22) | copy-start | bytes 98308
  108.3 112.1 %copy-start.7 = (f32[4096]{0:T(1024)S(1)}, f32[4096]{0:T(1024)}, u32[]{:S(2)}) copy-start(f32[4096]{0:T(1024)} %param.23) | copy-start | bytes 49156
  433.4 4.5 copy-start
  433.4 4.5 copy-start.2
  442.0 1.9 copy-start.3
  446.7 4.5 copy-start
  446.7 4.5 copy-start.2
  455.3 1.9 copy-start.3
  460.0 4.5 copy-start
  460.0 4.5 copy-start.2
  468.6 1.9 copy-start.3
  473.3 4.5 copy-start
  473.3 4.5 copy-start.2
  481.9 1.9 copy-start.3
Sparse Core Ops, SparseCore 0:
  483.9 130.6 all-reduce.1
where the time goes:
time: 626 us; the launch traced here: 625 us
  blocking collectives  285 us (46%)
  matrix products  180 us (29%)
  waiting for transfers between devices  71.2 us (11%)
  local copies, waits for them, and re-layouts  57.6 us (9%)
  other arithmetic  16.5 us (3%)
  between operations  14.2 us (2%)
    psum x2, blocking collectives, shards(): lax.psum(lax.fori_loop(0, slot_limit, col_advance, col_start).reshape(-1)...  116 us
    psum x2, blocking collectives, shards(): lax.psum(lax.fori_loop(0, slot_limit, row_advance, row_start).reshape(-1)...  109 us
    psum x1, waiting for transfers between devices, shards(): num_whole, den_whole = lax.psum((numerator, denominator), 'col')  71.2 us
    dot_general x20, matrix products, slot_kernel(): jnp.einsum('bad,bcd->bac', token_blocks, picked, preferred_element_type=j...  69.1 us
    psum x1, blocking collectives, shards(): num_whole, den_whole = lax.psum((numerator, denominator), 'col')  59.6 us
    dot_general x8, matrix products, col_advance(): jnp.einsum('bac,ba->bc', gibbs_similarity_matrix, col_source_square_numbe...  57.1 us
    gather x20, local copies, waits for them, and re-layouts, slot_kernel(): picked = jnp.take(centroid_blocks, chosen, axis=0)  42.7 us
    dot_general x8, matrix products, row_advance(): jnp.einsum('bac,bc->ba', gibbs_similarity_matrix, scales, precision=lax.P...  35.5 us
  transfers between devices with their start and end apart: 1, of which 1 were waited for; matrix products, arithmetic and copies ran while one was open for 0% of the time, Pallas kernels for 0%

commit v1 on v0

v1 whole, which is shorter than its diff:
```python
import functools
import math

import jax
import jax.numpy as jnp
from jax import lax
from jax.experimental import pallas as pl
from jax.experimental.pallas import tpu as pltpu
from jax.sharding import PartitionSpec as P

TILE = 128
SLOTS = 4
ITERS = 2
EPS = 0.025
OFFSET = 0.5
MESH = pl.DeviceIdType.MESH
F32 = jnp.float32
BF16 = jnp.bfloat16
NT = (((1,), (1,)), ((), ()))
TN = (((0,), (0,)), ((), ()))


def unit(values):
    wide = values.astype(F32)
    factor = lax.rsqrt(jnp.mean(wide * wide, axis=-1, keepdims=True) + 1e-06)
    return (wide * factor).astype(BF16)


def spread(row, rows=16):
    return jnp.broadcast_to(row, (rows, TILE)).astype(BF16)


def column(row):
    return jnp.transpose(jnp.broadcast_to(row, (TILE, TILE)))


def remote(src, dst, ss, rs, where):
    copy = pltpu.make_async_remote_copy(
        src_ref=src, dst_ref=dst, send_sem=ss, recv_sem=rs, device_id=where, device_id_type=MESH
    )
    copy.start()
    return copy


def wait_bytes(ref, sem):
    pltpu.make_async_copy(ref, ref, sem).wait()


def kernel(
    nrow, nz, tiles, local, qt,
    cand, cnt, tok, cen, rmass, cmass,
    qd, cd, out,
    cu, kb, cc, hot, psum, pair, zrow, rsc, qsum, crow, csc,
    pd, dpair, dsum, drow, nb, npair, fr, br,
    row_s, col_s, d_s, np_s, np_r, ring_s, ring_r, ag_s, ag_r, sh_s, sh_r,
):
    half = tiles // 2
    hq = qt // 2
    r = lax.axis_index("row")
    k = lax.axis_index("col")
    z = k // 2
    c = k % 2
    o = 1 - c
    partner = {"col": 2 * z + o}
    up = {"col": 2 * lax.rem(z + 1, nz) + c}
    down = {"col": 2 * lax.rem(z + nz - 1, nz) + c}

    barrier = pltpu.get_barrier_semaphore()
    pl.semaphore_signal(barrier, inc=1, device_id=partner, device_id_type=MESH)
    for d in range(1, nz):
        pl.semaphore_signal(
            barrier, inc=1, device_id={"col": 2 * lax.rem(z + d, nz) + c}, device_id_type=MESH
        )
    for d in range(1, nrow):
        pl.semaphore_signal(barrier, inc=1, device_id={"row": lax.rem(r + d, nrow)}, device_id_type=MESH)

    @pl.loop(0, local)
    def _(n):
        at = pl.ds(pl.multiple_of(n * TILE, TILE), TILE)
        cu[n] = unit(cen[at, :])

    lane = lax.broadcasted_iota(jnp.int32, (1, TILE), 1)
    ones = jnp.ones((16, TILE), BF16)
    scale = math.log2(math.e) / (TILE * EPS)
    shift = -OFFSET / EPS * math.log2(math.e)

    for h in range(2):

        @pl.loop(0, half)
        def _(g):
            t = h * half + g
            tu = unit(tok[pl.ds(pl.multiple_of(t * TILE, TILE), TILE), :])
            listed = cnt[t, 0]
            total = None
            for s in range(SLOTS):
                chosen = cand[t, s]
                sim = lax.dot_general(tu, cu[chosen], NT, preferred_element_type=F32)
                base = jnp.minimum(listed - (s + 1), 0).astype(F32) * 1e30 + shift
                gibbs = jnp.exp2(sim * scale + base)
                kb[t, :, s * TILE : (s + 1) * TILE] = gibbs.astype(BF16)
                total = gibbs if total is None else total + gibbs
                hot[s, pl.ds(t, 1), :] = (lane == chosen).astype(F32)
            sums = lax.dot_general(ones, total.astype(BF16), NT, preferred_element_type=F32)
            psum[0, h, pl.ds(g, 1), :] = sums[0:1, :]

    pl.semaphore_wait(barrier, nz + nrow - 1)

    def row_exchange(i):
        remote(psum.at[i, o], pair.at[i], row_s.at[i, 0], row_s.at[i, 1], partner).wait()
        zrow[i, z] = (psum[i, c] + pair[i]).astype(BF16)
        for d in range(1, nz):
            there = {"col": 2 * lax.rem(z + d, nz) + c}
            remote(zrow.at[i, z], zrow.at[i, z], row_s.at[i, 2], row_s.at[i, 3], there)
        wait_bytes(zrow.at[i, pl.ds(0, nz - 1)], row_s.at[i, 3])
        wait_bytes(zrow.at[i, pl.ds(0, nz - 1)], row_s.at[i, 2])
        whole = zrow[i, 0].astype(F32)
        for d in range(1, nz):
            whole = whole + zrow[i, d].astype(F32)
        rsc[i, c] = rmass[c] / whole
        remote(rsc.at[i, c], rsc.at[i, c], row_s.at[i, 4], row_s.at[i, 5], partner).wait()

    def col_exchange(i):
        for d in range(1, nrow):
            remote(crow.at[i, r], crow.at[i, r], col_s.at[i, 0], col_s.at[i, 1], {"row": lax.rem(r + d, nrow)})
        wait_bytes(crow.at[i, pl.ds(0, nrow - 1)], col_s.at[i, 1])
        wait_bytes(crow.at[i, pl.ds(0, nrow - 1)], col_s.at[i, 0])
        whole = crow[i, 0].astype(F32)
        for d in range(1, nrow):
            whole = whole + crow[i, d].astype(F32)
        csc[i] = cmass[...] / whole

    for i in range(ITERS):
        if i > 0:
            scales = jnp.concatenate([csc[i - 1], jnp.zeros((TILE - local, TILE), F32)], axis=0).astype(BF16)
            for s in range(SLOTS):
                qsum[s] = jnp.dot(hot[s].astype(BF16), scales, preferred_element_type=F32)
            for h in range(2):

                @pl.loop(0, half)
                def _(g):
                    t = h * half + g
                    sums = None
                    for s in range(SLOTS):
                        weight = spread(qsum[s, pl.ds(t, 1), :])
                        part = lax.dot_general(
                            weight, kb[t, :, s * TILE : (s + 1) * TILE], NT, preferred_element_type=F32
                        )
                        sums = part if sums is None else sums + part
                    psum[i, h, pl.ds(g, 1), :] = sums[0:1, :]

        row_exchange(i)

        for h in range(2):

            @pl.loop(0, half)
            def _(g):
                t = h * half + g
                weight = spread(rsc[i, h, pl.ds(g, 1), :])
                sums = jnp.dot(weight, kb[t], preferred_element_type=F32)
                for s in range(SLOTS):
                    qsum[s, pl.ds(t, 1), :] = sums[0:1, s * TILE : (s + 1) * TILE]

        whole = jnp.zeros((TILE, TILE), F32)
        for s in range(SLOTS):
            pick = hot[s].astype(BF16)
            high = qsum[s].astype(BF16)
            low = (qsum[s] - high.astype(F32)).astype(BF16)
            whole = whole + lax.dot_general(pick, high, TN, preferred_element_type=F32)
            whole = whole + lax.dot_general(pick, low, TN, preferred_element_type=F32)
        crow[i, r] = whole[0:local, :].astype(BF16)
        col_exchange(i)

    last = ITERS - 1

    @pl.loop(0, local)
    def _(n):
        wide = column(csc[last, pl.ds(n, 1), :] * (1.0 / 16.0))
        cc[n, :, 0:TILE] = (wide * cu[n].astype(F32)).astype(BF16)
        cc[n, :, TILE : 2 * TILE] = wide.astype(BF16)

    diagonal = lax.broadcasted_iota(jnp.int32, (TILE, TILE), 0) == lax.broadcasted_iota(
        jnp.int32, (TILE, TILE), 1
    )

    def numerators(h, g):
        for q in range(qt):
            t = h * half + g * qt + q
            acc = None
            for s in range(SLOTS):
                part = jnp.dot(
                    kb[t, :, s * TILE : (s + 1) * TILE], cc[cand[t, s]], preferred_element_type=F32
                )
                acc = part if acc is None else acc + part
            nb[h, g, q] = acc[:, 0:TILE].astype(BF16)
            mass = jnp.where(diagonal, acc[:, TILE : 2 * TILE], 0.0)
            pd[h, g, q : q + 1, :] = jnp.sum(mass, axis=0, keepdims=True)

    def group(d):
        return lax.rem(z + d, nz)

    sends = []
    far = nz // 2

    order = [far] + [x for j in range(1, far) for x in (far - j, far + j)] + [0]

    def give(j):
        return remote(nb.at[o, group(order[j])], npair.at[group(order[j])], np_s.at[j], np_r.at[j], partner)

    numerators(o, group(far))
    sends.append(give(0))
    numerators(c, group(far))

    def take(j):
        pltpu.make_async_copy(npair.at[0], npair.at[0], np_r.at[j]).wait()

    take(0)
    g = group(far)
    for q in range(qt):
        nb[c, g, q] = (nb[c, g, q].astype(F32) + npair[g, q].astype(F32)).astype(BF16)
    sends.append(remote(nb.at[c, g, pl.ds(0, hq)], fr.at[0, pl.ds(0, hq)], ring_s.at[0, 0, 0], ring_r.at[0, 0, 0], up))
    sends.append(remote(nb.at[c, g, pl.ds(hq, hq)], br.at[0, pl.ds(hq, hq)], ring_s.at[1, 0, 1], ring_r.at[1, 0, 1], down))

    for j in range(1, nz):
        numerators(o, group(order[j]))
        sends.append(give(j))

    @pl.loop(1, nz)
    def _(j):
        numerators(c, lax.rem(z + far + j, nz))

    copy = remote(pd.at[o], dpair, d_s.at[0], d_s.at[1], partner)
    copy.wait()
    dsum[...] = pd[c] + dpair[...]
    drow[z] = dsum[z]
    for d in range(1, nz):
        remote(dsum.at[group(d)], drow.at[z], d_s.at[2], d_s.at[3], {"col": 2 * group(d) + c})

    for step in range(1, far):
        for side, d, buf, to in ((0, far - step, fr, up), (1, far + step, br, down)):
            take(order.index(d))
        for part in range(2):
            for side, d, buf, to in ((0, far - step, fr, up), (1, far + step, br, down)):
                g = group(d)
                came = step > 1 or part == side
                if came:
                    ref = buf.at[step - 1, pl.ds(part * hq, hq)]
                    wait_bytes(ref, ring_r.at[side, step - 1, part])
                for q in range(part * hq, (part + 1) * hq):
                    value = nb[c, g, q].astype(F32) + npair[g, q].astype(F32)
                    if came:
                        value = value + buf[step - 1, q].astype(F32)
                    nb[c, g, q] = value.astype(BF16)
                sends.append(
                    remote(
                        nb.at[c, g, pl.ds(part * hq, hq)], buf.at[step, pl.ds(part * hq, hq)],
                        ring_s.at[side, step, part], ring_r.at[side, step, part], to,
                    )
                )

    wait_bytes(drow.at[pl.ds(0, nz - 1)], d_s.at[3])
    wait_bytes(drow.at[pl.ds(0, nz - 1)], d_s.at[2])
    mass = drow[0]
    for d in range(1, nz):
        mass = mass + drow[d]

    take(order.index(0))
    final = far - 1
    for part in range(2):
        mine = pl.ds(part * hq, hq)
        wait_bytes(fr.at[final, mine], ring_r.at[0, final, part])
        wait_bytes(br.at[final, mine], ring_r.at[1, final, part])
        for q in range(part * hq, (part + 1) * hq):
            value = nb[c, z, q].astype(F32) + npair[z, q].astype(F32)
            value = value + fr[final, q].astype(F32) + br[final, q].astype(F32)
            out[c, z, q] = (value / column(mass[q : q + 1, :])).astype(BF16)
        ref = out.at[c, z, mine]
        sends.append(remote(ref, ref, ag_s.at[0, 0, part], ag_r.at[0, 0, part], up))
        sends.append(remote(ref, ref, ag_s.at[1, 0, part], ag_r.at[1, 0, part], down))
        sends.append(remote(ref, ref, sh_s.at[0, 0, part], sh_r, partner))

    for dist in range(1, far + 1):
        for part in range(2):
            for side, g, to in ((0, group(nz - dist), up), (1, group(dist), down)):
                if dist == far and part != side:
                    continue
                ref = out.at[c, g, pl.ds(part * hq, hq)]
                wait_bytes(ref, ag_r.at[side, dist - 1, part])
                if dist < far - 1 or (dist == far - 1 and part == side):
                    sends.append(remote(ref, ref, ag_s.at[side, dist, part], ag_r.at[side, dist, part], to))
                sends.append(remote(ref, ref, sh_s.at[side, dist, part], sh_r, partner))

    qd[...] = EPS * jnp.log(rsc[last])
    cd[...] = EPS * jnp.log(csc[last])

    wait_bytes(out.at[o], sh_r)
    for copy in sends:
        copy.wait_send()


def shards(nrow, nz, tokens, centroids, row_mass, col_mass, candidates, counts):
    tiles = tokens.shape[0] // TILE
    local = centroids.shape[0] // TILE
    half = tiles // 2
    qt = half // nz
    far = nz // 2
    vmem = pl.BlockSpec(memory_space=pltpu.VMEM)
    smem = pl.BlockSpec(memory_space=pltpu.SMEM)
    dma = pltpu.SemaphoreType.DMA
    qd, cd, out = pl.pallas_call(
        functools.partial(kernel, nrow, nz, tiles, local, qt),
        out_shape=(
            jax.ShapeDtypeStruct((2, half, TILE), F32),
            jax.ShapeDtypeStruct((local, TILE), F32),
            jax.ShapeDtypeStruct((2, nz, qt, TILE, TILE), BF16),
        ),
        in_specs=[smem, smem, vmem, vmem, vmem, vmem],
        out_specs=(vmem, vmem, vmem),
        scratch_shapes=[
            pltpu.VMEM((local, TILE, TILE), BF16),
            pltpu.VMEM((tiles, TILE, SLOTS * TILE), BF16),
            pltpu.VMEM((local, TILE, 2 * TILE), BF16),
            pltpu.VMEM((SLOTS, tiles, TILE), F32),
            pltpu.VMEM((ITERS, 2, half, TILE), F32),
            pltpu.VMEM((ITERS, half, TILE), F32),
            pltpu.VMEM((ITERS, nz, half, TILE), BF16),
            pltpu.VMEM((ITERS, 2, half, TILE), F32),
            pltpu.VMEM((SLOTS, tiles, TILE), F32),
            pltpu.VMEM((ITERS, nrow, local, TILE), BF16),
            pltpu.VMEM((ITERS, local, TILE), F32),
            pltpu.VMEM((2, nz, qt, TILE), F32),
            pltpu.VMEM((nz, qt, TILE), F32),
            pltpu.VMEM((nz, qt, TILE), F32),
            pltpu.VMEM((nz, qt, TILE), F32),
            pltpu.VMEM((2, nz, qt, TILE, TILE), BF16),
            pltpu.VMEM((nz, qt, TILE, TILE), BF16),
            pltpu.VMEM((far, qt, TILE, TILE), BF16),
            pltpu.VMEM((far, qt, TILE, TILE), BF16),
            dma((ITERS, 6)),
            dma((ITERS, 2)),
            dma((4,)),
            dma((nz,)),
            dma((nz,)),
            dma((2, far, 2)),
            dma((2, far, 2)),
            dma((2, far + 1, 2)),
            dma((2, far + 1, 2)),
            dma((2, far + 1, 2)),
            dma(()),
        ],
        compiler_params=pltpu.CompilerParams(
            collective_id=0, has_side_effects=True, vmem_limit_bytes=48 << 20
        ),
    )(
        candidates, counts, tokens, centroids,
        row_mass.reshape(2, half, TILE), col_mass.reshape(local, TILE),
    )
    return qd.reshape(-1), cd.reshape(-1), out.reshape(tokens.shape)


def solution(mesh):
    in_specs = (
        P("row", None),
        P("col", None),
        P("row"),
        P("col"),
        P("row", "col"),
        P("row", "col"),
    )
    out_specs = (P("row"), P("col"), P("row", None))
    body = functools.partial(shards, mesh.shape["row"], mesh.shape["col"] // 2)
    return jax.shard_map(body, mesh=mesh, in_specs=in_specs, out_specs=out_specs, check_vma=False)
```

time: 626 us -> 144 us (0.23)
  blocking collectives: 285 us -> 0 us
  matrix products: 180 us -> 0 us
  Pallas kernels: 0 us -> 135 us
  waiting for transfers between devices: 71.2 us -> 0 us
  local copies, waits for them, and re-layouts: 57.6 us -> 8.35 us
  other arithmetic: 16.5 us -> 0 us
  between operations: 14.2 us -> 0.64 us
    psum x5 -> x0, blocking collectives: 285 us -> none  [the longest x2 116 us: shards(): lax.psum(lax.fori_loop(0, slot_limit, col_advance, col_start).reshape(-1)...]
    dot_general x48 -> x0, matrix products: 180 us -> none  [the longest x20 69.1 us: slot_kernel(): jnp.einsum('bad,bcd->bac', token_blocks, picked, preferred_element_type=j...]
    pallas_call x0 -> x1, Pallas kernels: none -> 135 us  [shards(): pl.pallas_call(functools.partial(kernel, nrow, nz, tiles, local, qt), out...]
    psum x1 -> x0, waiting for transfers between devices: 71.2 us -> none  [shards(): num_whole, den_whole = lax.psum((numerator, denominator), 'col')]
    gather x32 -> x0, local copies, waits for them, and re-layouts: 49.9 us -> none  [the longest x20 42.7 us: slot_kernel(): picked = jnp.take(centroid_blocks, chosen, axis=0)]
    convert_element_type x3 -> x0, other arithmetic: 9.04 us -> none  [the longest x2 5.23 us: unit_rows(): return (widened * factor).astype(jnp.bfloat16)]
    unnamed x10 -> x13, local copies, waits for them, and re-layouts: 0.03 us -> 8.35 us
    while x24 -> x0, local copies, waits for them, and re-layouts: 7.64 us -> none
  transfers between devices with their start and end apart: 1 -> 0, of which waited for: 1 -> 0; matrix products, arithmetic and copies ran while one was open for 0% -> 0% of each run, Pallas kernels for 0% -> 0%
where the time goes in v1:
time: 144 us
  Pallas kernels  135 us (94%)
  local copies, waits for them, and re-layouts  8.35 us (6%)
    pallas_call x1, Pallas kernels, shards(): pl.pallas_call(functools.partial(kernel, nrow, nz, tiles, local, qt), out...  135 us
    unnamed x13, local copies, waits for them, and re-layouts  8.35 us

profile of v1, /device:TPU:1, one launch (start us, length us, event | category | flops | bytes accessed | tf_op | source)
XLA Modules:
  0.0 144.0 jit_solution(10061015497352457018)
XLA Ops:
  0.6 0.8 copy.9.cand
  1.4 0.7 copy.10.cnt
  2.1 0.0 copy-start
  2.1 1.6 %copy-done = bf16[8192,128]{1,0:T(8,128)(2,1)S(1)} copy-done((bf16[8192,128]{1,0:T(8,128)(2,1)S(1)}, bf16[8192,128]{1,0:T(8,128)(2,1)}, u32[]{:S(2)}) %copy-start) | copy-done | bytes 2097176
  3.7 0.0 copy-start.1
  3.7 1.2 copy-done.1
  5.0 0.0 copy-start.2
  5.0 0.8 copy-done.2
  5.7 0.0 copy-start.3
  5.7 0.7 copy-done.3
  6.4 135.0 %shard_map.85 = (f32[2,32,128]{2,1,0:T(8,128)S(1)}, f32[32,128]{1,0:T(8,128)S(1)}, bf16[2,8,4,128,128]{4,3,2,1,0:T(8,128)(2,1)S(1)}) custom-call(s32[64,4]{1,0:T(8,128)S(1)} %copy.9.cand, s32[64,1]{1,0:T(8,128)S(1)} %copy.10.cnt, bf16[8192,128]{1,0:T(8,128)(2,1)S(1)} %copy-done, bf16[4096,128]{1,0:T(8,128)(2,1)S(1)} %copy-done.1, f32[2,32,128]{2,1,0:T(8,128)S(1)} %bitcast.6, ...), custom_call_target="tpu_custom_call" | custom-call | tf_op jit(solution)/shard_map/pallas_call | solution.py:309
  141.4 0.6 copy.14
  142.0 0.6 copy.15
  142.6 1.3 copy.16
Async XLA Ops:
  2.1 1.6 %copy-start = (bf16[8192,128]{1,0:T(8,128)(2,1)S(1)}, bf16[8192,128]{1,0:T(8,128)(2,1)}, u32[]{:S(2)}) copy-start(bf16[8192,128]{1,0:T(8,128)(2,1)} %tok.1) | copy-start | bytes 6291460
  3.7 1.2 copy-start.1
  5.0 0.8 copy-start.2
  5.7 0.7 copy-start.3

commit v2 on v1

v2 whole, which is shorter than its diff:
```python
import functools
import math

import jax
import jax.numpy as jnp
from jax import lax
from jax.experimental import pallas as pl
from jax.experimental.pallas import tpu as pltpu
from jax.sharding import PartitionSpec as P

TILE = 128
SLOTS = 4
ITERS = 2
CHUNKS = 8
EPS = 0.025
OFFSET = 0.5
MESH = pl.DeviceIdType.MESH
F32 = jnp.float32
BF16 = jnp.bfloat16
NT = (((1,), (1,)), ((), ()))
TN = (((0,), (0,)), ((), ()))


def unit(values):
    wide = values.astype(F32)
    factor = lax.rsqrt(jnp.mean(wide * wide, axis=-1, keepdims=True) + 1e-06)
    return (wide * factor).astype(BF16)


def spread(row, rows=16):
    return jnp.broadcast_to(row, (rows, TILE)).astype(BF16)


def column(row):
    return jnp.transpose(jnp.broadcast_to(row, (TILE, TILE)))


def remote(src, dst, ss, rs, where):
    copy = pltpu.make_async_remote_copy(
        src_ref=src, dst_ref=dst, send_sem=ss, recv_sem=rs, device_id=where, device_id_type=MESH
    )
    copy.start()
    return copy


def wait_bytes(ref, sem):
    pltpu.make_async_copy(ref, ref, sem).wait()


def kernel(
    nrow, nz, tiles, local, qt,
    cand, cnt, tok, cen, rmass, cmass,
    qd, cd, out,
    tokv, cenv, cu, kb, cc, hot, psum, pair, zrow, rsc, qsum, crow, csc,
    pd, dpair, dsum, drow, nb, npair, fr, br,
    in_s, row_s, col_s, d_s, d_r, np_s, np_r, ring_s, ring_r, ag_s, ag_r, sh_s, sh_r,
):
    half = tiles // 2
    hq = qt // 2
    r = lax.axis_index("row")
    k = lax.axis_index("col")
    z = k // 2
    c = k % 2
    o = 1 - c
    partner = {"col": 2 * z + o}
    up = {"col": 2 * lax.rem(z + 1, nz) + c}
    down = {"col": 2 * lax.rem(z + nz - 1, nz) + c}

    barrier = pltpu.get_barrier_semaphore()
    pl.semaphore_signal(barrier, inc=1, device_id=partner, device_id_type=MESH)
    for d in range(1, nz):
        pl.semaphore_signal(
            barrier, inc=1, device_id={"col": 2 * lax.rem(z + d, nz) + c}, device_id_type=MESH
        )
    for d in range(1, nrow):
        pl.semaphore_signal(barrier, inc=1, device_id={"row": lax.rem(r + d, nrow)}, device_id_type=MESH)

    chunk = tiles // CHUNKS
    load = pltpu.make_async_copy(cen, cenv, in_s.at[CHUNKS])
    load.start()
    for n in range(CHUNKS):
        at = pl.ds(n * chunk, chunk)
        pltpu.make_async_copy(tok.at[at], tokv.at[at], in_s.at[n]).start()

    load.wait()

    @pl.loop(0, local, unroll=4)
    def _(n):
        cu[n] = unit(cenv[n])

    lane = lax.broadcasted_iota(jnp.int32, (1, TILE), 1)
    scale = math.log2(math.e) / (TILE * EPS)
    shift = -OFFSET / EPS * math.log2(math.e)

    @pl.loop(0, CHUNKS)
    def _(n):
        at = pl.ds(n * chunk, chunk)
        pltpu.make_async_copy(tok.at[at], tokv.at[at], in_s.at[n]).wait()

        @pl.loop(0, chunk, unroll=8)
        def _(m):
            t = n * chunk + m
            tu = unit(tokv[t])
            listed = cnt[0, t]
            chosen = [cand[s, t] for s in range(SLOTS)]
            picked = jnp.concatenate([cu[x] for x in chosen], axis=0)
            sims = lax.dot_general(tu, picked, NT, preferred_element_type=F32)
            total = None
            for s in range(SLOTS):
                base = jnp.minimum(listed - (s + 1), 0).astype(F32) * 1e30 + shift
                gibbs = jnp.exp2(sims[:, s * TILE : (s + 1) * TILE] * scale + base)
                kb[t, :, s * TILE : (s + 1) * TILE] = gibbs.astype(BF16)
                total = gibbs if total is None else total + gibbs
                hot[s, pl.ds(t, 1), :] = (lane == chosen[s]).astype(F32)
            sums = jnp.transpose(jnp.sum(total, axis=1, keepdims=True))
            psum[0, n // (CHUNKS // 2), pl.ds(lax.rem(t, half), 1), :] = sums

    pl.semaphore_wait(barrier, nz + nrow - 1)

    def row_exchange(i):
        remote(psum.at[i, o], pair.at[i], row_s.at[i, 0], row_s.at[i, 1], partner).wait()
        zrow[i, z] = (psum[i, c] + pair[i]).astype(BF16)
        for d in range(1, nz):
            there = {"col": 2 * lax.rem(z + d, nz) + c}
            remote(zrow.at[i, z], zrow.at[i, z], row_s.at[i, 2], row_s.at[i, 3], there)
        wait_bytes(zrow.at[i, pl.ds(0, nz - 1)], row_s.at[i, 3])
        wait_bytes(zrow.at[i, pl.ds(0, nz - 1)], row_s.at[i, 2])
        whole = zrow[i, 0].astype(F32)
        for d in range(1, nz):
            whole = whole + zrow[i, d].astype(F32)
        rsc[i, c] = rmass[c] / whole
        remote(rsc.at[i, c], rsc.at[i, c], row_s.at[i, 4], row_s.at[i, 5], partner).wait()

    def col_exchange(i):
        for d in range(1, nrow):
            remote(crow.at[i, r], crow.at[i, r], col_s.at[i, 0], col_s.at[i, 1], {"row": lax.rem(r + d, nrow)})
        wait_bytes(crow.at[i, pl.ds(0, nrow - 1)], col_s.at[i, 1])
        wait_bytes(crow.at[i, pl.ds(0, nrow - 1)], col_s.at[i, 0])
        whole = crow[i, 0].astype(F32)
        for d in range(1, nrow):
            whole = whole + crow[i, d].astype(F32)
        csc[i] = cmass[...] / whole

    for i in range(ITERS):
        if i > 0:
            scales = jnp.concatenate([csc[i - 1], jnp.zeros((TILE - local, TILE), F32)], axis=0).astype(BF16)
            for s in range(SLOTS):
                qsum[s] = jnp.dot(hot[s].astype(BF16), scales, preferred_element_type=F32)
            for h in range(2):

                @pl.loop(0, half, unroll=8)
                def _(g):
                    t = h * half + g
                    weight = jnp.concatenate([spread(qsum[s, pl.ds(t, 1), :]) for s in range(SLOTS)], axis=1)
                    sums = lax.dot_general(weight, kb[t], NT, preferred_element_type=F32)
                    psum[i, h, pl.ds(g, 1), :] = sums[0:1, :]

        row_exchange(i)

        for h in range(2):

            @pl.loop(0, half, unroll=8)
            def _(g):
                t = h * half + g
                weight = spread(rsc[i, h, pl.ds(g, 1), :])
                sums = jnp.dot(weight, kb[t], preferred_element_type=F32)
                for s in range(SLOTS):
                    qsum[s, pl.ds(t, 1), :] = sums[0:1, s * TILE : (s + 1) * TILE]

        whole = jnp.zeros((TILE, TILE), F32)
        for s in range(SLOTS):
            pick = hot[s].astype(BF16)
            high = qsum[s].astype(BF16)
            low = (qsum[s] - high.astype(F32)).astype(BF16)
            whole = whole + lax.dot_general(pick, high, TN, preferred_element_type=F32)
            whole = whole + lax.dot_general(pick, low, TN, preferred_element_type=F32)
        crow[i, r] = whole[0:local, :].astype(BF16)
        col_exchange(i)

    last = ITERS - 1

    @pl.loop(0, local, unroll=4)
    def _(n):
        wide = column(csc[last, pl.ds(n, 1), :] * (1.0 / 16.0))
        cc[n, :, 0:TILE] = (wide * cu[n].astype(F32)).astype(BF16)
        cc[n, :, TILE : 2 * TILE] = wide.astype(BF16)

    diagonal = lax.broadcasted_iota(jnp.int32, (TILE, TILE), 0) == lax.broadcasted_iota(
        jnp.int32, (TILE, TILE), 1
    )

    def numerators(h, g):
        for q in range(qt):
            t = h * half + g * qt + q
            scaled = jnp.concatenate([cc[cand[s, t]] for s in range(SLOTS)], axis=0)
            acc = jnp.dot(kb[t], scaled, preferred_element_type=F32)
            nb[h, g, q] = acc[:, 0:TILE].astype(BF16)
            mass = jnp.where(diagonal, acc[:, TILE : 2 * TILE], 0.0)
            pd[h, g, q : q + 1, :] = jnp.sum(mass, axis=0, keepdims=True)

    def group(d):
        return lax.rem(z + d, nz)

    sends = []
    far = nz // 2
    order = [far] + [x for j in range(1, far) for x in (far - j, far + j)] + [0]

    def give(d):
        j, g = order.index(d), group(d)
        numerators(o, g)
        sends.append(remote(nb.at[o, g], npair.at[g], np_s.at[j], np_r.at[j], partner))
        sends.append(remote(pd.at[o, g], dpair.at[g], d_s.at[0, j], d_r.at[j], partner))

    def take(d):
        j, g = order.index(d), group(d)
        wait_bytes(npair.at[g], np_r.at[j])
        wait_bytes(dpair.at[g], d_r.at[j])
        dsum[g] = pd[c, g] + dpair[g]
        if d == 0:
            drow[z] = dsum[z]
        else:
            sends.append(remote(dsum.at[g], drow.at[z], d_s.at[1, j], d_r.at[nz], {"col": 2 * g + c}))

    def ring(side, step, q):
        buf, to = ((fr, up), (br, down))[side]
        g = group(far - step if side == 0 else far + step)
        value = nb[c, g, q].astype(F32) + npair[g, q].astype(F32)
        if step > 1 or (step == 1 and (q < hq) == (side == 0)):
            wait_bytes(buf.at[step - 1, q], ring_r.at[side, step - 1, q])
            value = value + buf[step - 1, q].astype(F32)
        nb[c, g, q] = value.astype(BF16)
        sends.append(
            remote(nb.at[c, g, q], buf.at[step, q], ring_s.at[side, step, q], ring_r.at[side, step, q], to)
        )

    first, second = list(range(hq)), list(range(hq, qt))
    give(far)
    numerators(c, group(far))
    give(far - 1)
    take(far)
    for a, b in zip(first, second):
        ring(0, 0, a)
        ring(1, 0, b)
    for step in range(1, far):
        if step > 1:
            give(far - step)
        give(far + step)
        numerators(c, group(far - step))
        numerators(c, group(far + step))
        if step == far - 1:
            give(0)
        take(far - step)
        take(far + step)
        for a, b in zip(second + first, first + second):
            ring(0, step, a)
            ring(1, step, b)
    numerators(c, z)
    take(0)

    wait_bytes(drow.at[pl.ds(0, nz - 1)], d_r.at[nz])
    mass = drow[0]
    for d in range(1, nz):
        mass = mass + drow[d]

    final = far - 1
    for q in range(qt):
        value = nb[c, z, q].astype(F32) + npair[z, q].astype(F32)
        scale_out = 1.0 / column(mass[q : q + 1, :])
        wait_bytes(fr.at[final, q], ring_r.at[0, final, q])
        wait_bytes(br.at[final, q], ring_r.at[1, final, q])
        value = value + fr[final, q].astype(F32) + br[final, q].astype(F32)
        out[c, z, q] = (value * scale_out).astype(BF16)
        ref = out.at[c, z, q]
        sends.append(remote(ref, ref, ag_s.at[0, 0, q], ag_r.at[0, 0, q], up))
        sends.append(remote(ref, ref, ag_s.at[1, 0, q], ag_r.at[1, 0, q], down))
        sends.append(remote(ref, ref, sh_s.at[0, 0, q], sh_r, partner))

    for dist in range(1, far + 1):
        for q in range(qt):
            for side, g, to in ((0, group(nz - dist), up), (1, group(dist), down)):
                longest = (q < hq) == (side == 0)
                if dist == far and not longest:
                    continue
                ref = out.at[c, g, q]
                wait_bytes(ref, ag_r.at[side, dist - 1, q])
                if dist < far - 1 or (dist == far - 1 and longest):
                    sends.append(remote(ref, ref, ag_s.at[side, dist, q], ag_r.at[side, dist, q], to))
                sends.append(remote(ref, ref, sh_s.at[side, dist, q], sh_r, partner))

    qd[...] = EPS * jnp.log(rsc[last])
    cd[...] = EPS * jnp.log(csc[last])

    wait_bytes(out.at[o], sh_r)
    for copy in sends:
        copy.wait_send()


def shards(nrow, nz, tokens, centroids, row_mass, col_mass, candidates, counts):
    tiles = tokens.shape[0] // TILE
    local = centroids.shape[0] // TILE
    half = tiles // 2
    qt = half // nz
    far = nz // 2
    vmem = pl.BlockSpec(memory_space=pltpu.VMEM)
    hbm = pl.BlockSpec(memory_space=pl.ANY)
    smem = pl.BlockSpec(memory_space=pltpu.SMEM)
    dma = pltpu.SemaphoreType.DMA
    qd, cd, out = pl.pallas_call(
        functools.partial(kernel, nrow, nz, tiles, local, qt),
        out_shape=(
            jax.ShapeDtypeStruct((2, half, TILE), F32),
            jax.ShapeDtypeStruct((local, TILE), F32),
            jax.ShapeDtypeStruct((2, nz, qt, TILE, TILE), BF16),
        ),
        in_specs=[smem, smem, hbm, hbm, vmem, vmem],
        out_specs=(vmem, vmem, vmem),
        scratch_shapes=[
            pltpu.VMEM((tiles, TILE, TILE), BF16),
            pltpu.VMEM((local, TILE, TILE), BF16),
            pltpu.VMEM((local, TILE, TILE), BF16),
            pltpu.VMEM((tiles, TILE, SLOTS * TILE), BF16),
            pltpu.VMEM((local, TILE, 2 * TILE), BF16),
            pltpu.VMEM((SLOTS, tiles, TILE), F32),
            pltpu.VMEM((ITERS, 2, half, TILE), F32),
            pltpu.VMEM((ITERS, half, TILE), F32),
            pltpu.VMEM((ITERS, nz, half, TILE), BF16),
            pltpu.VMEM((ITERS, 2, half, TILE), F32),
            pltpu.VMEM((SLOTS, tiles, TILE), F32),
            pltpu.VMEM((ITERS, nrow, local, TILE), BF16),
            pltpu.VMEM((ITERS, local, TILE), F32),
            pltpu.VMEM((2, nz, qt, TILE), F32),
            pltpu.VMEM((nz, qt, TILE), F32),
            pltpu.VMEM((nz, qt, TILE), F32),
            pltpu.VMEM((nz, qt, TILE), F32),
            pltpu.VMEM((2, nz, qt, TILE, TILE), BF16),
            pltpu.VMEM((nz, qt, TILE, TILE), BF16),
            pltpu.VMEM((far, qt, TILE, TILE), BF16),
            pltpu.VMEM((far, qt, TILE, TILE), BF16),
            dma((CHUNKS + 1,)),
            dma((ITERS, 6)),
            dma((ITERS, 2)),
            dma((2, nz)),
            dma((nz + 1,)),
            dma((nz,)),
            dma((nz,)),
            dma((2, far, qt)),
            dma((2, far, qt)),
            dma((2, far + 1, qt)),
            dma((2, far + 1, qt)),
            dma((2, far + 1, qt)),
            dma(()),
        ],
        compiler_params=pltpu.CompilerParams(
            collective_id=0, has_side_effects=True, vmem_limit_bytes=60 << 20
        ),
    )(
        candidates.T, counts.T,
        tokens.reshape(tiles, TILE, TILE), centroids.reshape(local, TILE, TILE),
        row_mass.reshape(2, half, TILE), col_mass.reshape(local, TILE),
    )
    return qd.reshape(-1), cd.reshape(-1), out.reshape(tokens.shape)


def solution(mesh):
    in_specs = (
        P("row", None),
        P("col", None),
        P("row"),
        P("col"),
        P("row", "col"),
        P("row", "col"),
    )
    out_specs = (P("row"), P("col"), P("row", None))
    body = functools.partial(shards, mesh.shape["row"], mesh.shape["col"] // 2)
    return jax.shard_map(body, mesh=mesh, in_specs=in_specs, out_specs=out_specs, check_vma=False)
```

time: 144 us -> 92.8 us (0.64)
  Pallas kernels: 135 us -> 86.1 us
  local copies, waits for them, and re-layouts: 8.35 us -> 5.74 us
    pallas_call x1, Pallas kernels: 135 us -> 86.1 us  [shards(): pl.pallas_call(functools.partial(kernel, nrow, nz, tiles, local, qt), out...]
    unnamed x13 -> x3, local copies, waits for them, and re-layouts: 8.35 us -> 5.74 us
where the time goes in v2:
time: 92.8 us; the launch traced here: 92.5 us
  Pallas kernels  86.1 us (93%)
  local copies, waits for them, and re-layouts  5.74 us (6%)
    pallas_call x1, Pallas kernels, shards(): pl.pallas_call(functools.partial(kernel, nrow, nz, tiles, local, qt), out...  86.1 us
    unnamed x3, local copies, waits for them, and re-layouts  5.74 us

profile of v2, /device:TPU:1, one launch (start us, length us, event | category | flops | bytes accessed | tf_op | source)
XLA Modules:
  0.0 92.5 jit_solution(4113978627213805643)
XLA Ops:
  0.6 86.1 %shard_map.85 = (f32[2,32,128]{2,1,0:T(8,128)}, f32[32,128]{1,0:T(8,128)}, bf16[2,8,4,128,128]{4,3,2,1,0:T(8,128)(2,1)}) custom-call(s32[4,64]{1,0:T(4,128)} %bitcast.16, s32[1,64]{1,0:T(1,128)} %bitcast.17, bf16[64,128,128]{2,1,0:T(8,128)(2,1)} %bitcast.9, bf16[32,128,128]{2,1,0:T(8,128)(2,1)} %bitcast.11, f32[2,32,128]{2,1,0:T(8,128)} %bitcast.12, ...), custom_call_target="tpu_custom_call" | custom-call | tf_op jit(solution)/shard_map/pallas_call | solution.py:308
  86.7 1.4 %copy.12 = f32[8192]{0:T(1024)} copy(f32[8192]{0:T(1024)} %bitcast.13) | data formatting | bytes 65536
  88.1 1.3 %copy.13 = f32[4096]{0:T(1024)} copy(f32[4096]{0:T(1024)} %bitcast.15) | data formatting | bytes 32768
  89.4 3.0 %copy.14 = bf16[8192,128]{1,0:T(8,128)(2,1)} copy(bf16[8192,128]{1,0:T(8,128)(2,1)} %bitcast.10) | data formatting | bytes 4194304

commit v3 on v2

--- a/solution.py
+++ b/solution.py
@@ -65,6 +65,8 @@
     partner = {"col": 2 * z + o}
     up = {"col": 2 * lax.rem(z + 1, nz) + c}
     down = {"col": 2 * lax.rem(z + nz - 1, nz) + c}
+    up2 = {"col": 2 * lax.rem(z + 2, nz) + c}
+    down2 = {"col": 2 * lax.rem(z + nz - 2, nz) + c}
 
     barrier = pltpu.get_barrier_semaphore()
     pl.semaphore_signal(barrier, inc=1, device_id=partner, device_id_type=MESH)
@@ -222,12 +224,16 @@
             sends.append(remote(dsum.at[g], drow.at[z], d_s.at[1, j], d_r.at[nz], {"col": 2 * g + c}))
 
     def ring(side, step, q):
-        buf, to = ((fr, up), (br, down))[side]
+        buf = (fr, br)[side]
+        to = ((up2, down2) if step == 0 else (up, down))[side]
         g = group(far - step if side == 0 else far + step)
         value = nb[c, g, q].astype(F32) + npair[g, q].astype(F32)
-        if step > 1 or (step == 1 and (q < hq) == (side == 0)):
-            wait_bytes(buf.at[step - 1, q], ring_r.at[side, step - 1, q])
-            value = value + buf[step - 1, q].astype(F32)
+        came = [step - 1] if step > 1 else []
+        if step == 2 and (q < hq) == (side == 0):
+            came.append(0)
+        for n in came:
+            wait_bytes(buf.at[n, q], ring_r.at[side, n, q])
+            value = value + buf[n, q].astype(F32)
         nb[c, g, q] = value.astype(BF16)
         sends.append(
             remote(nb.at[c, g, q], buf.at[step, q], ring_s.at[side, step, q], ring_r.at[side, step, q], to)
@@ -273,19 +279,28 @@
         ref = out.at[c, z, q]
         sends.append(remote(ref, ref, ag_s.at[0, 0, q], ag_r.at[0, 0, q], up))
         sends.append(remote(ref, ref, ag_s.at[1, 0, q], ag_r.at[1, 0, q], down))
-        sends.append(remote(ref, ref, sh_s.at[0, 0, q], sh_r, partner))
-
+
+    def share(n, ref):
+        sends.append(remote(ref, ref, sh_s.at[n], sh_r, partner))
+
+    share(0, out.at[c, z])
     for dist in range(1, far + 1):
         for q in range(qt):
-            for side, g, to in ((0, group(nz - dist), up), (1, group(dist), down)):
+            for side, g, to, to2 in ((0, group(nz - dist), up, up2), (1, group(dist), down, down2)):
                 longest = (q < hq) == (side == 0)
                 if dist == far and not longest:
                     continue
                 ref = out.at[c, g, q]
                 wait_bytes(ref, ag_r.at[side, dist - 1, q])
-                if dist < far - 1 or (dist == far - 1 and longest):
+                if dist == far - 2 and longest:
+                    sends.append(remote(ref, ref, ag_s.at[side, far - 1, q], ag_r.at[side, far - 1, q], to2))
+                if dist < far - 1:
                     sends.append(remote(ref, ref, ag_s.at[side, dist, q], ag_r.at[side, dist, q], to))
-                sends.append(remote(ref, ref, sh_s.at[side, dist, q], sh_r, partner))
+        if dist < far:
+            share(2 * dist - 1, out.at[c, group(nz - dist)])
+            share(2 * dist, out.at[c, group(dist)])
+        else:
+            share(2 * far - 1, out.at[c, group(far)])
 
     qd[...] = EPS * jnp.log(rsc[last])
     cd[...] = EPS * jnp.log(csc[last])
@@ -302,7 +317,7 @@
     qt = half // nz
     far = nz // 2
     vmem = pl.BlockSpec(memory_space=pltpu.VMEM)
-    hbm = pl.BlockSpec(memory_space=pl.ANY)
+    hbm = pl.BlockSpec(memory_space=pltpu.HBM)
     smem = pl.BlockSpec(memory_space=pltpu.SMEM)
     dma = pltpu.SemaphoreType.DMA
     qd, cd, out = pl.pallas_call(
@@ -345,18 +360,23 @@
             dma((nz,)),
             dma((2, far, qt)),
             dma((2, far, qt)),
-            dma((2, far + 1, qt)),
-            dma((2, far + 1, qt)),
-            dma((2, far + 1, qt)),
+            dma((2, far, qt)),
+            dma((2, far, qt)),
+            dma((nz,)),
             dma(()),
         ],
         compiler_params=pltpu.CompilerParams(
-            collective_id=0, has_side_effects=True, vmem_limit_bytes=60 << 20
+            collective_id=0, has_side_effects=True, vmem_limit_bytes=36 << 20
         ),
     )(
-        candidates.T, counts.T,
-        tokens.reshape(tiles, TILE, TILE), centroids.reshape(local, TILE, TILE),
-        row_mass.reshape(2, half, TILE), col_mass.reshape(local, TILE),
+        *(
+            pltpu.with_memory_space_constraint(x, pltpu.HBM)
+            for x in (
+                candidates.T, counts.T,
+                tokens.reshape(tiles, TILE, TILE), centroids.reshape(local, TILE, TILE),
+                row_mass.reshape(2, half, TILE), col_mass.reshape(local, TILE),
+            )
+        )
     )
     return qd.reshape(-1), cd.reshape(-1), out.reshape(tokens.shape)
 

time: 92.8 us -> 87.3 us (0.941)
  local copies, waits for them, and re-layouts: 5.74 us -> 2.54 us
  Pallas kernels: 86.1 us -> 84 us
    unnamed x3, local copies, waits for them, and re-layouts: 5.74 us -> 2.54 us
    pallas_call x1, Pallas kernels: 86.1 us -> 84 us  [shards(): pl.pallas_call(functools.partial(kernel, nrow, nz, tiles, local, qt), out...]
where the time goes in v3:
time: 87.3 us; the launch traced here: 87.2 us
  Pallas kernels  84 us (96%)
  local copies, waits for them, and re-layouts  2.54 us (3%)
    pallas_call x1, Pallas kernels, shards(): pl.pallas_call(functools.partial(kernel, nrow, nz, tiles, local, qt), out...  84 us
    unnamed x3, local copies, waits for them, and re-layouts  2.54 us

profile of v3, /device:TPU:1, one launch (start us, length us, event | category | flops | bytes accessed | tf_op | source)
XLA Modules:
  0.0 87.2 jit_solution(9623243540582762751)
XLA Ops:
  0.6 84.0 %shard_map.85 = (f32[2,32,128]{2,1,0:T(8,128)S(1)}, f32[32,128]{1,0:T(8,128)S(1)}, bf16[2,8,4,128,128]{4,3,2,1,0:T(8,128)(2,1)S(1)}) custom-call(s32[4,64]{1,0:T(4,128)} %bitcast.16, s32[1,64]{1,0:T(1,128)} %bitcast.17, bf16[64,128,128]{2,1,0:T(8,128)(2,1)} %bitcast.12, bf16[32,128,128]{2,1,0:T(8,128)(2,1)} %bitcast.13, f32[2,32,128]{2,1,0:T(8,128)} %bitcast.14, ...), custom_call_target="tpu_custom_call" | custom-call | tf_op jit(solution)/shard_map/pallas_call | solution.py:323
  84.6 0.6 copy.12
  85.3 0.6 copy.13
  85.9 1.3 %copy.14 = bf16[8192,128]{1,0:T(8,128)(2,1)} copy(bf16[8192,128]{1,0:T(8,128)(2,1)S(1)} %bitcast.9) | data formatting | bytes 4194304

commit v4 on v3

--- a/solution.py
+++ b/solution.py
@@ -51,7 +51,7 @@
     nrow, nz, tiles, local, qt,
     cand, cnt, tok, cen, rmass, cmass,
     qd, cd, out,
-    tokv, cenv, cu, kb, cc, hot, psum, pair, zrow, rsc, qsum, crow, csc,
+    tokv, cenv, rmv, cmv, cu, kb, cc, hot, psum, pair, zrow, rsc, qsum, crow, csc,
     pd, dpair, dsum, drow, nb, npair, fr, br,
     in_s, row_s, col_s, d_s, d_r, np_s, np_r, ring_s, ring_r, ag_s, ag_r, sh_s, sh_r,
 ):
@@ -80,9 +80,16 @@
     chunk = tiles // CHUNKS
     load = pltpu.make_async_copy(cen, cenv, in_s.at[CHUNKS])
     load.start()
-    for n in range(CHUNKS):
-        at = pl.ds(n * chunk, chunk)
-        pltpu.make_async_copy(tok.at[at], tokv.at[at], in_s.at[n]).start()
+    for h in (o, c):
+        for n in range(CHUNKS // 2):
+            at = pl.ds(h * half + n * chunk, chunk)
+            pltpu.make_async_copy(tok.at[at], tokv.at[at], in_s.at[h * (CHUNKS // 2) + n]).start()
+    masses = [
+        pltpu.make_async_copy(rmass, rmv, in_s.at[CHUNKS + 1]),
+        pltpu.make_async_copy(cmass, cmv, in_s.at[CHUNKS + 2]),
+    ]
+    for copy in masses:
+        copy.start()
 
     load.wait()
 
@@ -94,44 +101,57 @@
     scale = math.log2(math.e) / (TILE * EPS)
     shift = -OFFSET / EPS * math.log2(math.e)
 
-    @pl.loop(0, CHUNKS)
-    def _(n):
-        at = pl.ds(n * chunk, chunk)
-        pltpu.make_async_copy(tok.at[at], tokv.at[at], in_s.at[n]).wait()
-
-        @pl.loop(0, chunk, unroll=8)
-        def _(m):
-            t = n * chunk + m
-            tu = unit(tokv[t])
-            listed = cnt[0, t]
-            chosen = [cand[s, t] for s in range(SLOTS)]
-            picked = jnp.concatenate([cu[x] for x in chosen], axis=0)
-            sims = lax.dot_general(tu, picked, NT, preferred_element_type=F32)
-            total = None
-            for s in range(SLOTS):
-                base = jnp.minimum(listed - (s + 1), 0).astype(F32) * 1e30 + shift
-                gibbs = jnp.exp2(sims[:, s * TILE : (s + 1) * TILE] * scale + base)
-                kb[t, :, s * TILE : (s + 1) * TILE] = gibbs.astype(BF16)
-                total = gibbs if total is None else total + gibbs
-                hot[s, pl.ds(t, 1), :] = (lane == chosen[s]).astype(F32)
-            sums = jnp.transpose(jnp.sum(total, axis=1, keepdims=True))
-            psum[0, n // (CHUNKS // 2), pl.ds(lax.rem(t, half), 1), :] = sums
-
-    pl.semaphore_wait(barrier, nz + nrow - 1)
-
-    def row_exchange(i):
-        remote(psum.at[i, o], pair.at[i], row_s.at[i, 0], row_s.at[i, 1], partner).wait()
+    def fill(h):
+        @pl.loop(0, CHUNKS // 2)
+        def _(n):
+            first = h * half + n * chunk
+            at = pl.ds(first, chunk)
+            pltpu.make_async_copy(tok.at[at], tokv.at[at], in_s.at[h * (CHUNKS // 2) + n]).wait()
+
+            @pl.loop(0, chunk, unroll=8)
+            def _(m):
+                one_tile(h, n * chunk + m, first + m)
+
+    def one_tile(h, g, t):
+        tu = unit(tokv[t])
+        listed = cnt[0, t]
+        chosen = [cand[s, t] for s in range(SLOTS)]
+        picked = jnp.concatenate([cu[x] for x in chosen], axis=0)
+        sims = lax.dot_general(tu, picked, NT, preferred_element_type=F32)
+        total = None
+        for s in range(SLOTS):
+            base = jnp.minimum(listed - (s + 1), 0).astype(F32) * 1e30 + shift
+            gibbs = jnp.exp2(sims[:, s * TILE : (s + 1) * TILE] * scale + base)
+            kb[t, :, s * TILE : (s + 1) * TILE] = gibbs.astype(BF16)
+            total = gibbs if total is None else total + gibbs
+            hot[s, pl.ds(t, 1), :] = (lane == chosen[s]).astype(F32)
+        sums = jnp.transpose(jnp.sum(total, axis=1, keepdims=True))
+        psum[0, h, pl.ds(g, 1), :] = sums
+
+    def row_send(i):
+        return remote(psum.at[i, o], pair.at[i], row_s.at[i, 0], row_s.at[i, 1], partner)
+
+    def row_exchange(i, sent):
+        sent.wait()
         zrow[i, z] = (psum[i, c] + pair[i]).astype(BF16)
         for d in range(1, nz):
             there = {"col": 2 * lax.rem(z + d, nz) + c}
             remote(zrow.at[i, z], zrow.at[i, z], row_s.at[i, 2], row_s.at[i, 3], there)
         wait_bytes(zrow.at[i, pl.ds(0, nz - 1)], row_s.at[i, 3])
-        wait_bytes(zrow.at[i, pl.ds(0, nz - 1)], row_s.at[i, 2])
         whole = zrow[i, 0].astype(F32)
         for d in range(1, nz):
             whole = whole + zrow[i, d].astype(F32)
-        rsc[i, c] = rmass[c] / whole
-        remote(rsc.at[i, c], rsc.at[i, c], row_s.at[i, 4], row_s.at[i, 5], partner).wait()
+        rsc[i, c] = rmv[c] / whole
+        shared = remote(rsc.at[i, c], rsc.at[i, c], row_s.at[i, 4], row_s.at[i, 5], partner)
+        wait_bytes(zrow.at[i, pl.ds(0, nz - 1)], row_s.at[i, 2])
+        return shared
+
+    fill(o)
+    pl.semaphore_wait(barrier, nz + nrow - 1)
+    sent = row_send(0)
+    fill(c)
+    for copy in masses:
+        copy.wait()
 
     def col_exchange(i):
         for d in range(1, nrow):
@@ -141,15 +161,15 @@
         whole = crow[i, 0].astype(F32)
         for d in range(1, nrow):
             whole = whole + crow[i, d].astype(F32)
-        csc[i] = cmass[...] / whole
+        csc[i] = cmv[...] / whole
 
     for i in range(ITERS):
         if i > 0:
             scales = jnp.concatenate([csc[i - 1], jnp.zeros((TILE - local, TILE), F32)], axis=0).astype(BF16)
             for s in range(SLOTS):
                 qsum[s] = jnp.dot(hot[s].astype(BF16), scales, preferred_element_type=F32)
-            for h in range(2):
-
+
+            def row_pass(h):
                 @pl.loop(0, half, unroll=8)
                 def _(g):
                     t = h * half + g
@@ -157,10 +177,13 @@
                     sums = lax.dot_general(weight, kb[t], NT, preferred_element_type=F32)
                     psum[i, h, pl.ds(g, 1), :] = sums[0:1, :]
 
-        row_exchange(i)
-
-        for h in range(2):
-
+            row_pass(o)
+            sent = row_send(i)
+            row_pass(c)
+
+        shared = row_exchange(i, sent)
+
+        def col_pass(h):
             @pl.loop(0, half, unroll=8)
             def _(g):
                 t = h * half + g
@@ -169,6 +192,9 @@
                 for s in range(SLOTS):
                     qsum[s, pl.ds(t, 1), :] = sums[0:1, s * TILE : (s + 1) * TILE]
 
+        col_pass(c)
+        shared.wait()
+        col_pass(o)
         whole = jnp.zeros((TILE, TILE), F32)
         for s in range(SLOTS):
             pick = hot[s].astype(BF16)
@@ -241,8 +267,9 @@
 
     first, second = list(range(hq)), list(range(hq, qt))
     give(far)
+    give(far - 1)
+    give(far + 1)
     numerators(c, group(far))
-    give(far - 1)
     take(far)
     for a, b in zip(first, second):
         ring(0, 0, a)
@@ -250,7 +277,7 @@
     for step in range(1, far):
         if step > 1:
             give(far - step)
-        give(far + step)
+            give(far + step)
         numerators(c, group(far - step))
         numerators(c, group(far + step))
         if step == far - 1:
@@ -327,11 +354,13 @@
             jax.ShapeDtypeStruct((local, TILE), F32),
             jax.ShapeDtypeStruct((2, nz, qt, TILE, TILE), BF16),
         ),
-        in_specs=[smem, smem, hbm, hbm, vmem, vmem],
+        in_specs=[smem, smem, hbm, hbm, hbm, hbm],
         out_specs=(vmem, vmem, vmem),
         scratch_shapes=[
             pltpu.VMEM((tiles, TILE, TILE), BF16),
             pltpu.VMEM((local, TILE, TILE), BF16),
+            pltpu.VMEM((2, half, TILE), F32),
+            pltpu.VMEM((local, TILE), F32),
             pltpu.VMEM((local, TILE, TILE), BF16),
             pltpu.VMEM((tiles, TILE, SLOTS * TILE), BF16),
             pltpu.VMEM((local, TILE, 2 * TILE), BF16),
@@ -351,7 +380,7 @@
             pltpu.VMEM((nz, qt, TILE, TILE), BF16),
             pltpu.VMEM((far, qt, TILE, TILE), BF16),
             pltpu.VMEM((far, qt, TILE, TILE), BF16),
-            dma((CHUNKS + 1,)),
+            dma((CHUNKS + 3,)),
             dma((ITERS, 6)),
             dma((ITERS, 2)),
             dma((2, nz)),

time: 87.3 us -> 83.6 us (0.958)
  Pallas kernels: 84 us -> 80.3 us
    pallas_call x1, Pallas kernels: 84 us -> 80.3 us  [shards(): pl.pallas_call(functools.partial(kernel, nrow, nz, tiles, local, qt), out...]
where the time goes in v4:
time: 83.6 us; the launch traced here: 83.5 us
  Pallas kernels  80.3 us (96%)
  local copies, waits for them, and re-layouts  2.54 us (3%)
    pallas_call x1, Pallas kernels, shards(): pl.pallas_call(functools.partial(kernel, nrow, nz, tiles, local, qt), out...  80.3 us
    unnamed x3, local copies, waits for them, and re-layouts  2.54 us

profile of v4, /device:TPU:1, one launch (start us, length us, event | category | flops | bytes accessed | tf_op | source)
XLA Modules:
  0.0 83.5 jit_solution(8705784574774048624)
XLA Ops:
  0.6 80.3 %shard_map.85 = (f32[2,32,128]{2,1,0:T(8,128)S(1)}, f32[32,128]{1,0:T(8,128)S(1)}, bf16[2,8,4,128,128]{4,3,2,1,0:T(8,128)(2,1)S(1)}) custom-call(s32[4,64]{1,0:T(4,128)} %bitcast.16, s32[1,64]{1,0:T(1,128)} %bitcast.17, bf16[64,128,128]{2,1,0:T(8,128)(2,1)} %bitcast.12, bf16[32,128,128]{2,1,0:T(8,128)(2,1)} %bitcast.13, f32[2,32,128]{2,1,0:T(8,128)} %bitcast.14, ...), custom_call_target="tpu_custom_call" | custom-call | tf_op jit(solution)/shard_map/pallas_call | solution.py:350
  80.9 0.6 copy.12
  81.5 0.6 copy.13
  82.1 1.3 %copy.14 = bf16[8192,128]{1,0:T(8,128)(2,1)} copy(bf16[8192,128]{1,0:T(8,128)(2,1)S(1)} %bitcast.9) | data formatting | bytes 4194304

commit v5 on v4

--- a/solution.py
+++ b/solution.py
@@ -134,7 +134,7 @@
     def row_exchange(i, sent):
         sent.wait()
         zrow[i, z] = (psum[i, c] + pair[i]).astype(BF16)
-        for d in range(1, nz):
+        for d in sorted(range(1, nz), key=lambda d: -min(d, nz - d)):
             there = {"col": 2 * lax.rem(z + d, nz) + c}
             remote(zrow.at[i, z], zrow.at[i, z], row_s.at[i, 2], row_s.at[i, 3], there)
         wait_bytes(zrow.at[i, pl.ds(0, nz - 1)], row_s.at[i, 3])
@@ -154,7 +154,9 @@
         copy.wait()
 
     def col_exchange(i):
-        for d in range(1, nrow):
+        side = math.isqrt(nrow)
+        hops = lambda d: min(d // side, side - d // side) + min(d % side, side - d % side)
+        for d in sorted(range(1, nrow), key=lambda d: -hops(d)):
             remote(crow.at[i, r], crow.at[i, r], col_s.at[i, 0], col_s.at[i, 1], {"row": lax.rem(r + d, nrow)})
         wait_bytes(crow.at[i, pl.ds(0, nrow - 1)], col_s.at[i, 1])
         wait_bytes(crow.at[i, pl.ds(0, nrow - 1)], col_s.at[i, 0])

time: 83.6 us -> 82.5 us (0.987)
  Pallas kernels: 80.3 us -> 79.2 us
    pallas_call x1, Pallas kernels: 80.3 us -> 79.2 us  [shards(): pl.pallas_call(functools.partial(kernel, nrow, nz, tiles, local, qt), out...]
where the time goes in v5:
time: 82.5 us; the launch traced here: 82.4 us
  Pallas kernels  79.2 us (96%)
  local copies, waits for them, and re-layouts  2.54 us (3%)
    pallas_call x1, Pallas kernels, shards(): pl.pallas_call(functools.partial(kernel, nrow, nz, tiles, local, qt), out...  79.2 us
    unnamed x3, local copies, waits for them, and re-layouts  2.54 us

profile of v5, /device:TPU:1, one launch (start us, length us, event | category | flops | bytes accessed | tf_op | source)
XLA Modules:
  0.0 82.4 jit_solution(6768849402803965064)
XLA Ops:
  0.6 79.2 %shard_map.85 = (f32[2,32,128]{2,1,0:T(8,128)S(1)}, f32[32,128]{1,0:T(8,128)S(1)}, bf16[2,8,4,128,128]{4,3,2,1,0:T(8,128)(2,1)S(1)}) custom-call(s32[4,64]{1,0:T(4,128)} %bitcast.16, s32[1,64]{1,0:T(1,128)} %bitcast.17, bf16[64,128,128]{2,1,0:T(8,128)(2,1)} %bitcast.12, bf16[32,128,128]{2,1,0:T(8,128)(2,1)} %bitcast.13, f32[2,32,128]{2,1,0:T(8,128)} %bitcast.14, ...), custom_call_target="tpu_custom_call" | custom-call | tf_op jit(solution)/shard_map/pallas_call | solution.py:352
  79.8 0.6 copy.12
  80.4 0.6 copy.13
  81.0 1.3 %copy.14 = bf16[8192,128]{1,0:T(8,128)(2,1)} copy(bf16[8192,128]{1,0:T(8,128)(2,1)S(1)} %bitcast.9) | data formatting | bytes 4194304
